TPU v7x, 32 devices: a whole 2x2x4 slice. The times are simulated.
32 devices in a mesh: sub: 8 (over y, x, core), row: 4 (over z).
Axes of the slice: x: 2, y: 2, z: 4, core: 2. Of those that a mesh axis runs over, the one named last changes fastest.
Arguments:
- sigma_top: float32 [6144, 6144], P('row', 'sub'), may hold values from -2 to 4, as said below
- coupling: float32 [8, 6144, 768], P('sub', 'row'), may hold values from -0.16 to 0.16
- child_inverse: float32 [8, 768, 768], P('sub', 'row'), may hold values from -1 to 10, as said below
- tile_mask: int32 [8, 24], P('sub'), may hold values 0 or 1
- obs_node: int32 [8192], P(('sub', 'row')), may hold values from 0 to 6143
- obs_noise: float32 [8192], P(('sub', 'row')), may hold values from 0.05 to 2
Outputs:
- sep_child: float32 [8, 6144, 768], P('sub', 'row')
- child_block: float32 [8, 768, 768], P('sub', 'row')
- loo_var: float32 [8192], P(('sub', 'row'))
Inputs may be any that keep to these rules, and one draw needn't show every extreme that they name: sigma_top is exactly symmetric. Each child_inverse[c] is exactly symmetric.
All inputs are finite; a program needn't handle non-finite values. No bound on the sum of `tile_mask` on one device may be relied on, other than what follows from the above.
Results may differ from a plain program's by a relative error of at most 0.000073.
Values sent between devices are 32-bit elements; how exact they have to be, the bound alone decides.
A program may use at most 128 MiB of HBM per device.

v0:
```python
import jax
import jax.numpy as jnp
from jax import lax
from jax.sharding import PartitionSpec as P

TILE = 256


def local(sigma_top, coupling, child_inverse, tile_mask, obs_node, obs_noise):
    highest = lax.Precision.HIGHEST
    rows_here = coupling.shape[1]
    width_here = child_inverse.shape[1]
    tiles_here = rows_here // TILE
    row_index = lax.axis_index("row")
    mask_here = lax.dynamic_slice_in_dim(tile_mask[0], row_index * tiles_here, tiles_here)
    row_mask = jnp.repeat(mask_here, TILE).astype(jnp.float32)
    masked = coupling[0] * row_mask[:, None]
    gathered = lax.all_gather(masked, "row", axis=0, tiled=True)
    product = jnp.dot(
        lax.all_gather(sigma_top, "sub", axis=1, tiled=True),
        gathered,
        precision=highest,
        preferred_element_type=jnp.float32,
    )
    sep_part = -product
    update = lax.psum_scatter(
        lax.dot_general(
            masked,
            sep_part,
            (((0,), (0,)), ((), ())),
            precision=highest,
            preferred_element_type=jnp.float32,
        ),
        "row",
        scatter_dimension=0,
        tiled=True,
    )
    block_here = child_inverse[0] - update
    own_cols = lax.dynamic_slice_in_dim(block_here, row_index * width_here, width_here, 1)
    own_diag = jnp.diagonal(own_cols)
    every_var = lax.all_gather(own_diag, ("sub", "row"), axis=0, tiled=True)
    loo_var = every_var[obs_node] + obs_noise
    return (sep_part[None], block_here[None], loo_var)


def solution(mesh):
    placed = (
        P("row", "sub"),
        P("sub", "row", None),
        P("sub", "row", None),
        P("sub", None),
        P(("sub", "row")),
        P(("sub", "row")),
    )
    return jax.shard_map(
        local,
        mesh=mesh,
        in_specs=placed,
        out_specs=(P("sub", "row", None), P("sub", "row", None), P(("sub", "row"))),
        check_vma=False,
    )
```

profile of v0, /device:TPU:0, one launch (start us, length us, event | category | flops | bytes accessed | tf_op | source)
XLA Modules:
  0.0 833.6 jit_solution(15396792678136300137)
XLA Ops:
  7.2 0.0 all-gather.3.cloned.1.call-start
  7.2 0.7 convert_bitcast_fusion
  7.9 0.1 broadcast_in_dim.17
  8.0 4.9 bitcast_multiply_fusion
  12.9 0.0 all-gather.3.cloned.1.call-update
  12.9 0.0 all-gather.5.cloned.1.call-start
  13.0 0.7 all-gather.5.cloned.1.call-update
  13.7 0.0 reduce-scatter.2.cloned.1.call-start
  13.7 324.7 %all-gather.3.cloned.1.call-done = f32[6144,768]{1,0:T(8,128)} async-done(((f32[1536,768]{1,0:T(8,128)}), f32[6144,768]{1,0:T(8,128)}) %all-gather.3.cloned.1.call-update) | async-done | bytes 18874384 | tf_op jit(solution)/shard_map/all_gather | solution.py:18
  338.4 180.4 %all-gather.5.cloned.1.call-done = f32[1536,6144]{1,0:T(8,128)} async-done(((f32[1536,768]{1,0:T(8,128)}), f32[1536,6144]{1,0:T(8,128)}) %all-gather.5.cloned.1.call-update) | async-done | bytes 37748752 | tf_op jit(solution)/shard_map/all_gather | solution.py:20
  518.8 187.1 %fusion.2 = f32[768,1536]{1,0:T(8,128)S(1)} fusion(f32[6144,768]{1,0:T(8,128)} %all-gather.3.cloned.1.call-done, f32[1536,6144]{1,0:T(8,128)} %all-gather.5.cloned.1.call-done), kind=kOutput, calls=%fused_computation.12 | convolution fusion | flops 86973087744 | bytes 61341696 | tf_op jit(solution)/shard_map/dot_general | solution.py:19
  705.9 0.0 copy-start
  705.9 2.1 copy-done
  708.0 0.0 copy-start.4
  708.0 25.1 %fusion = f32[768,768]{1,0:T(8,128)} fusion(f32[1536,768]{1,0:T(8,128)} %bitcast_multiply_fusion, f32[768,1536]{1,0:T(8,128)S(1)} %fusion.2), kind=kOutput, calls=%fused_computation.3 | convolution fusion | flops 10872815616 | bytes 11796480 | tf_op jit(solution)/shard_map/dot_general | solution.py:27
  733.1 0.0 reduce-scatter.2.cloned.1.call-update
  733.1 0.0 copy-done.4
  733.2 5.0 negate_bitcast_fusion
  738.1 0.0 copy-start.2
  738.1 0.0 copy-start.3
  738.1 6.4 copy.10
  744.6 36.7 %reduce-scatter.2.cloned.1.call-done = f32[192,768]{1,0:T(8,128)} async-done(((f32[768,768]{1,0:T(8,128)}), f32[192,768]{1,0:T(8,128)}) %reduce-scatter.2.cloned.1.call-update) | async-done | bytes 589840 | tf_op jit(solution)/shard_map/reduce_scatter | solution.py:26
  781.3 0.0 copy-done.2
  781.3 1.1 bitcast_subtract_fusion
  782.4 0.0 copy-start.1
  782.5 0.1 constant_dynamic-slice_fusion
  782.6 1.9 gather_fusion
  784.5 0.3 dynamic-update-slice
  784.8 39.9 %all-reduce = f32[6144]{0:T(1024)S(1)} all-reduce(f32[6144]{0:T(1024)S(1)} %dynamic-update-slice), channel_id=1, replica_groups=mesh['sub'=8,'row'=4] {'sub','row'}, use_global_device_ids=true, to_apply=%add | all-reduce | flops 6144 | bytes 49152
  824.7 1.7 gather_fusion.1
  826.5 0.0 copy-done.3
  826.5 0.6 add.25
  827.0 0.0 copy-done.1
  (5 shorter events, 0.0 us)
Async XLA Ops:
  7.2 331.2 %all-gather.3.cloned.1.call-start = ((), (), s32[]{:S(2)}) async-start(), calls=%async_computation.1 | async-start | bytes 23592960 | tf_op jit(solution)/shard_map/all_gather | solution.py:18
  12.9 505.8 %all-gather.5.cloned.1.call-start = ((), (), s32[]{:S(2)}) async-start(), calls=%async_computation.2 | async-start | bytes 42467328 | tf_op jit(solution)/shard_map/all_gather | solution.py:20
  13.7 767.6 %reduce-scatter.2.cloned.1.call-start = ((), (), s32[]{:S(2)}) async-start(), calls=%async_computation.3 | async-start | bytes 2949120 | tf_op jit(solution)/shard_map/reduce_scatter | solution.py:26
  705.9 2.1 copy-start
  708.0 25.1 %copy-start.4 = (s32[256]{0:T(256)S(1)}, s32[256]{0:T(256)}, u32[]{:S(2)}) copy-start(s32[256]{0:T(256)} %param.10) | copy-start | bytes 3076
  738.1 43.2 %copy-start.2 = (f32[1,192,768]{2,1,0:T(8,128)S(1)}, f32[1,192,768]{2,1,0:T(8,128)}, u32[]{:S(2)}) copy-start(f32[1,192,768]{2,1,0:T(8,128)} %param.8) | copy-start | bytes 1769476
  738.1 88.3 %copy-start.3 = (f32[256]{0:T(256)S(1)}, f32[256]{0:T(256)}, u32[]{:S(2)}) copy-start(f32[256]{0:T(256)} %param.11) | copy-start | bytes 3076
  782.4 44.6 %copy-start.1 = (f32[192,768]{1,0:T(8,128)}, f32[192,768]{1,0:T(8,128)S(1)}, u32[]{:S(2)}) copy-start(f32[192,768]{1,0:T(8,128)S(1)} %bitcast_subtract_fusion) | copy-start | bytes 1769476
Sparse Core Ops, SparseCore 0:
  13.1 325.2 all-gather.2
  340.3 178.4 all-gather.4
  733.2 48.0 reduce-scatter.1
where the time goes:
time: 834 us
  waiting for transfers between devices  542 us (65%)
  matrix products  212 us (25%)
  blocking collectives  39.9 us (5%)
  between operations  13.9 us (2%)
  local copies, waits for them, and re-layouts  12.7 us (2%)
  other arithmetic  12.3 us (1%)
    all_gather x1, waiting for transfers between devices, local(): gathered = lax.all_gather(masked, 'row', axis=0, tiled=True)  325 us
    dot_general x1, matrix products, local(): jnp.dot(lax.all_gather(sigma_top, 'sub', axis=1, tiled=True), gathered, p...  187 us
    all_gather x1, waiting for transfers between devices, local(): lax.all_gather(sigma_top, 'sub', axis=1, tiled=True)  180 us
    unnamed x1, blocking collectives  39.9 us
    reduce_scatter x1, waiting for transfers between devices, local(): lax.psum_scatter(lax.dot_general(masked, sep_part, (((0,), (0,)), ((), ()...  36.7 us
    dot_general x1, matrix products, local(): lax.dot_general(masked, sep_part, (((0,), (0,)), ((), ())), precision=hig...  25.1 us
  transfers between devices with their start and end apart: 3, of which 3 were waited for; matrix products, arithmetic and copies ran while one was open for 1% of the time, Pallas kernels for 0%

commit v1 on v0

v1 whole, which is shorter than its diff:
```python
import functools
import jax
import jax.numpy as jnp
from jax import lax
from jax.experimental import pallas as pl
from jax.experimental.pallas import tpu as pltpu
from jax.sharding import PartitionSpec as P

TILE = 256
STRIP = 128
MESH = pl.DeviceIdType.MESH


def flip(index, bits, size):
    total, step = 0, 1
    while step < size:
        digit = (index // step) % 2
        if (bits // step) % 2:
            digit = 1 - digit
        total = total + digit * step
        step *= 2
    return total


def halves(x):
    high = x.astype(jnp.bfloat16)
    low = (x - high.astype(jnp.float32)).astype(jnp.bfloat16)
    return high, low


def gather_multiply(
    subs, rows, mask_ref, s_ref, m_ref, out_ref, s_all, m_all,
    s_tile, m_tile, m_high, m_low,
    s_send, s_pass, s_recv, m_up, m_down, m_recv, load_sem, own_sem,
):
    sub, row = lax.axis_index("sub"), lax.axis_index("row")
    chips = subs // 2
    chip, core = sub // 2, sub % 2
    mate = chip * 2 + (1 - core)
    height, depth = s_ref.shape
    per = height // depth
    strips = depth // STRIP
    rt = 512 if height % 512 == 0 else 256

    def peer(x):
        return flip(chip, x, chips) * 2 + core

    barrier = pltpu.get_barrier_semaphore()
    for x in range(1, chips):
        pl.semaphore_signal(barrier, inc=1, device_id=(peer(x), row), device_id_type=MESH)
    pl.semaphore_signal(barrier, inc=1, device_id=(mate, row), device_id_type=MESH)

    @pl.when(row > 0)
    def _():
        pl.semaphore_signal(barrier, inc=1, device_id=(sub, row - 1), device_id_type=MESH)

    @pl.when(row < rows - 1)
    def _():
        pl.semaphore_signal(barrier, inc=1, device_id=(sub, row + 1), device_id_type=MESH)

    @pl.when((row > 0) & (row < rows - 1))
    def _():
        pl.semaphore_wait(barrier, chips + 2)

    @pl.when((row == 0) | (row == rows - 1))
    def _():
        pl.semaphore_wait(barrier, chips + 1)

    def m_copy(src, j, up):
        return pltpu.make_async_remote_copy(
            src_ref=src, dst_ref=m_all.at[j],
            send_sem=(m_up if up else m_down).at[j], recv_sem=m_recv.at[j],
            device_id=(sub, row + 1 if up else row - 1), device_id_type=MESH,
        )

    def s_copy(x):
        return pltpu.make_async_remote_copy(
            src_ref=s_ref, dst_ref=s_all.at[sub],
            send_sem=s_send.at[x], recv_sem=s_recv.at[sub],
            device_id=(peer(x), row), device_id_type=MESH,
        )

    def s_pass_on(x):
        block = peer(x)
        return pltpu.make_async_remote_copy(
            src_ref=s_ref if x == 0 else s_all.at[block], dst_ref=s_all.at[block],
            send_sem=s_pass.at[x], recv_sem=s_recv.at[block],
            device_id=(mate, row), device_id_type=MESH,
        )

    def s_arrived(block):
        return pltpu.make_async_remote_copy(
            src_ref=s_all.at[block], dst_ref=s_all.at[block],
            send_sem=s_send.at[0], recv_sem=s_recv.at[block],
            device_id=(mate, row), device_id_type=MESH,
        )

    def m_arrived(j):
        return pltpu.make_async_remote_copy(
            src_ref=m_all.at[j], dst_ref=m_all.at[j],
            send_sem=m_up.at[j], recv_sem=m_recv.at[j],
            device_id=(mate, row), device_id_type=MESH,
        )

    for h in range(per):
        @pl.when(row < rows - 1)
        def _():
            m_copy(m_ref.at[h], row * per + h, True).start()

        @pl.when(row > 0)
        def _():
            m_copy(m_ref.at[h], row * per + h, False).start()
    for x in range(1, chips):
        s_copy(x).start()
    s_pass_on(0).start()

    own_s = pltpu.make_async_copy(s_ref, s_all.at[sub], own_sem.at[0])
    own_m = pltpu.make_async_copy(m_ref, m_all.at[pl.ds(row * per, per)], own_sem.at[1])
    own_s.start()
    own_m.start()
    out_ref[...] = jnp.zeros_like(out_ref)
    own_s.wait()
    own_m.wait()

    def receive(distance, h, then):
        for sign in (1, -1):
            block = row + sign * distance

            @pl.when((block >= 0) & (block < rows))
            def _():
                j = block * per + h
                m_arrived(j).wait_recv()
                if sign == 1:
                    @pl.when(row > 0)
                    def _():
                        m_copy(m_all.at[j], j, False).start()
                else:
                    @pl.when(row < rows - 1)
                    def _():
                        m_copy(m_all.at[j], j, True).start()
                if then is not None:
                    then(j)

    def multiply(j):
        load_s = pltpu.make_async_copy(s_all.at[j], s_tile, load_sem.at[0])
        load_m = pltpu.make_async_copy(m_all.at[j], m_tile, load_sem.at[1])
        load_s.start()
        load_m.start()
        load_m.wait()

        @pl.loop(0, strips)
        def _(i):
            part = pl.ds(pl.multiple_of(i * STRIP, STRIP), STRIP)
            high, low = halves(m_tile[part, :] * mask_ref[j * strips + i][0:1, :])
            m_high[part, :] = high
            m_low[part, :] = low

        load_s.wait()

        @pl.loop(0, height // rt)
        def _(i):
            part = pl.ds(pl.multiple_of(i * rt, rt), rt)
            high, low = halves(s_tile[part, :])
            out_ref[part, :] += (
                jnp.dot(high, m_low[...], preferred_element_type=jnp.float32)
                + jnp.dot(low, m_high[...], preferred_element_type=jnp.float32)
                + jnp.dot(high, m_high[...], preferred_element_type=jnp.float32)
            )

    near = min(2, rows - 2)
    for h in range(per):
        receive(1, h, None)
    for x in range(1, chips):
        s_arrived(peer(x)).wait_recv()
        s_pass_on(x).start()
    for distance in range(2, near + 1):
        for h in range(per):
            receive(distance, h, None)
    for x in range(chips):
        s_arrived(flip(chip, x, chips) * 2 + (1 - core)).wait_recv()

    @pl.loop(0, subs)
    def _(j):
        block = j // per

        @pl.when((block - row <= near) & (row - block <= near))
        def _():
            multiply(j)

    @pl.loop(0, (rows - 1 - near) * per)
    def _(n):
        receive(near + 1 + n // per, n % per, multiply)

    for x in range(1, chips):
        s_copy(x).wait_send()
    for x in range(chips):
        s_pass_on(x).wait_send()

    @pl.loop(0, subs)
    def _(j):
        block = j // per

        @pl.when((row < rows - 1) & (block <= row))
        def _():
            m_copy(m_all.at[j], j, True).wait_send()

        @pl.when((row > 0) & (block >= row))
        def _():
            m_copy(m_all.at[j], j, False).wait_send()


def product_here(subs, rows, sigma_top, coupling, tile_mask):
    height, depth = sigma_top.shape
    width = coupling.shape[1]
    per = height // depth
    f32 = jnp.float32
    strips = jnp.repeat(tile_mask, TILE // STRIP).astype(f32)
    strips = jnp.broadcast_to(strips[:, None, None], (strips.shape[0], 8, width))
    whole = pl.BlockSpec(memory_space=pltpu.VMEM)
    hbm = pl.BlockSpec(memory_space=pl.ANY)
    dma = pltpu.SemaphoreType.DMA
    return pl.pallas_call(
        functools.partial(gather_multiply, subs, rows),
        out_shape=(
            jax.ShapeDtypeStruct((height, width), f32),
            jax.ShapeDtypeStruct((subs, height, depth), f32),
            jax.ShapeDtypeStruct((subs, depth, width), f32),
        ),
        in_specs=[whole, hbm, hbm],
        out_specs=(whole, hbm, hbm),
        scratch_shapes=[
            pltpu.VMEM((height, depth), f32),
            pltpu.VMEM((depth, width), f32),
            pltpu.VMEM((depth, width), jnp.bfloat16),
            pltpu.VMEM((depth, width), jnp.bfloat16),
            dma((subs // 2,)),
            dma((subs // 2,)),
            dma((subs,)),
            dma((subs,)),
            dma((subs,)),
            dma((subs,)),
            dma((2,)),
            dma((2,)),
        ],
        compiler_params=pltpu.CompilerParams(
            collective_id=0, has_side_effects=True, vmem_limit_bytes=56 * 2**20
        ),
        cost_estimate=pl.CostEstimate(
            flops=6 * height * subs * depth * width,
            bytes_accessed=8 * (height + width) * subs * depth,
            transcendentals=0,
        ),
    )(strips, sigma_top, coupling.reshape(per, depth, width))[0]


def local(subs, rows, sigma_top, coupling, child_inverse, tile_mask, obs_node, obs_noise):
    rows_here = coupling.shape[1]
    width_here = child_inverse.shape[1]
    tiles_here = rows_here // TILE
    row_index = lax.axis_index("row")
    mask_here = lax.dynamic_slice_in_dim(tile_mask[0], row_index * tiles_here, tiles_here)
    row_mask = jnp.repeat(mask_here, TILE).astype(jnp.float32)
    masked = coupling[0] * row_mask[:, None]
    sep_part = -product_here(subs, rows, sigma_top, coupling[0], tile_mask[0])
    update = lax.psum_scatter(
        lax.dot_general(
            masked,
            sep_part,
            (((0,), (0,)), ((), ())),
            precision=lax.Precision.HIGH,
            preferred_element_type=jnp.float32,
        ),
        "row",
        scatter_dimension=0,
        tiled=True,
    )
    block_here = child_inverse[0] - update
    own_cols = lax.dynamic_slice_in_dim(block_here, row_index * width_here, width_here, 1)
    own_diag = jnp.diagonal(own_cols)
    every_var = lax.all_gather(own_diag, ("sub", "row"), axis=0, tiled=True)
    loo_var = every_var[obs_node] + obs_noise
    return (sep_part[None], block_here[None], loo_var)


def solution(mesh):
    placed = (
        P("row", "sub"),
        P("sub", "row", None),
        P("sub", "row", None),
        P("sub", None),
        P(("sub", "row")),
        P(("sub", "row")),
    )
    return jax.shard_map(
        functools.partial(local, mesh.shape["sub"], mesh.shape["row"]),
        mesh=mesh,
        in_specs=placed,
        out_specs=(P("sub", "row", None), P("sub", "row", None), P(("sub", "row"))),
        check_vma=False,
    )
```

time: 834 us -> 630 us (0.76)
  Pallas kernels: 0 us -> 509 us
  waiting for transfers between devices: 542 us -> 42.5 us
  matrix products: 212 us -> 10.8 us
    pallas_call x0 -> x1, Pallas kernels: none -> 509 us  [product_here(): pl.pallas_call(functools.partial(gather_multiply, subs, rows), out_shape=...]
    all_gather x2 -> x0, waiting for transfers between devices: 505 us -> none  [the longest x1 325 us: local(): gathered = lax.all_gather(masked, 'row', axis=0, tiled=True)]
    dot_general x2 -> x1, matrix products: 212 us -> 10.8 us  [local(): lax.dot_general(masked, sep_part, (((0,), (0,)), ((), ())), precision=lax...]
    unnamed x13 -> x12, local copies, waits for them, and re-layouts: 8.85 us -> 0.31 us
  transfers between devices with their start and end apart: 3 -> 1, of which waited for: 3 -> 1; matrix products, arithmetic and copies ran while one was open for 1% -> 1% of each run, Pallas kernels for 0% -> 0%
where the time goes in v1:
time: 630 us
  Pallas kernels  509 us (81%)
  waiting for transfers between devices  42.5 us (7%)
  blocking collectives  39.9 us (6%)
  between operations  14.2 us (2%)
  matrix products  10.8 us (2%)
  other arithmetic  8 us (1%)
    pallas_call x1, Pallas kernels, product_here(): pl.pallas_call(functools.partial(gather_multiply, subs, rows), out_shape=...  509 us
    reduce_scatter x1, waiting for transfers between devices, local(): lax.psum_scatter(lax.dot_general(masked, sep_part, (((0,), (0,)), ((), ()...  42.5 us
    unnamed x1, blocking collectives  39.9 us
  transfers between devices with their start and end apart: 1, of which 1 were waited for; matrix products, arithmetic and copies ran while one was open for 1% of the time, Pallas kernels for 0%

profile of v1, /device:TPU:0, one launch (start us, length us, event | category | flops | bytes accessed | tf_op | source)
XLA Modules:
  0.0 630.1 jit_solution(16451640598155063769)
XLA Ops:
  7.2 0.0 reduce-scatter.2.cloned.1.call-start
  7.2 0.7 convert_bitcast_fusion.1
  7.9 0.1 broadcast_in_dim.26
  7.9 0.1 convert_element_type.30
  8.0 0.7 convert_bitcast_fusion
  8.8 0.1 broadcast_in_dim.29
  8.9 1.2 broadcast_in_dim.27.mask_ref
  10.0 0.0 copy-start.4
  10.0 509.3 %shard_map.85 = (f32[1536,768]{1,0:T(8,128)}, f32[8,1536,768]{2,1,0:T(8,128)}, f32[8,768,768]{2,1,0:T(8,128)}) custom-call(f32[48,8,768]{2,1,0:T(8,128)} %broadcast_in_dim.27.mask_ref, f32[1536,768]{1,0:T(8,128)} %s_ref.1, f32[2,768,768]{2,1,0:T(8,128)} %bitcast.16), custom_call_target="tpu_custom_call" | custom-call | flops 43486543872 | bytes 113246208 | tf_op jit(solution)/shard_map/pallas_call | solution.py:222
  519.3 0.0 copy-done.4
  519.3 0.0 copy-start.3
  519.3 10.8 %fusion = f32[768,768]{1,0:T(8,128)} fusion(f32[1,1536,768]{2,1,0:T(8,128)S(1)} %copy-done.4, f32[1536,768]{1,0:T(8,128)} %get-tuple-element.4, f32[1536]{0:T(1024)S(1)} %convert_element_type.33), kind=kOutput, calls=%fused_computation.3 | convolution fusion | flops 5438177280 | bytes 11802624 | tf_op jit(solution)/shard_map/dot_general | solution.py:266
  530.1 0.0 reduce-scatter.2.cloned.1.call-update
  530.1 0.0 copy-done.3
  530.1 0.0 copy-start.1
  530.1 0.0 copy-start.2
  530.2 4.9 negate_bitcast_fusion
  535.0 42.5 %reduce-scatter.2.cloned.1.call-done = f32[192,768]{1,0:T(8,128)} async-done(((f32[768,768]{1,0:T(8,128)}), f32[192,768]{1,0:T(8,128)}) %reduce-scatter.2.cloned.1.call-update) | async-done | bytes 589840 | tf_op jit(solution)/shard_map/reduce_scatter | solution.py:265
  577.5 0.0 copy-done.1
  577.5 1.1 bitcast_subtract_fusion
  578.7 0.0 copy-start
  578.7 0.1 constant_dynamic-slice_fusion
  578.8 1.9 gather_fusion
  580.8 0.3 dynamic-update-slice
  581.0 39.9 %all-reduce = f32[6144]{0:T(1024)S(1)} all-reduce(f32[6144]{0:T(1024)S(1)} %dynamic-update-slice), channel_id=1, replica_groups=mesh['sub'=8,'row'=4] {'sub','row'}, use_global_device_ids=true, to_apply=%add | all-reduce | flops 6144 | bytes 49152
  621.0 1.7 gather_fusion.1
  622.7 0.0 copy-done.2
  622.7 0.6 add.25
  623.3 0.0 copy-done
  (5 shorter events, 0.0 us)
Async XLA Ops:
  7.2 570.4 %reduce-scatter.2.cloned.1.call-start = ((), (), s32[]{:S(2)}) async-start(), calls=%async_computation.1 | async-start | bytes 2949120 | tf_op jit(solution)/shard_map/reduce_scatter | solution.py:265
  10.0 509.3 %copy-start.4 = (f32[1,1536,768]{2,1,0:T(8,128)S(1)}, f32[1,1536,768]{2,1,0:T(8,128)}, u32[]{:S(2)}) copy-start(f32[1,1536,768]{2,1,0:T(8,128)} %param.7) | copy-start | bytes 14155780
  519.3 10.8 %copy-start.3 = (s32[256]{0:T(256)S(1)}, s32[256]{0:T(256)}, u32[]{:S(2)}) copy-start(s32[256]{0:T(256)} %param.10) | copy-start | bytes 3076
  530.1 47.4 %copy-start.1 = (f32[1,192,768]{2,1,0:T(8,128)S(1)}, f32[1,192,768]{2,1,0:T(8,128)}, u32[]{:S(2)}) copy-start(f32[1,192,768]{2,1,0:T(8,128)} %param.8) | copy-start | bytes 1769476
  530.1 92.5 %copy-start.2 = (f32[256]{0:T(256)S(1)}, f32[256]{0:T(256)}, u32[]{:S(2)}) copy-start(f32[256]{0:T(256)} %param.11) | copy-start | bytes 3076
  578.7 44.6 %copy-start = (f32[192,768]{1,0:T(8,128)}, f32[192,768]{1,0:T(8,128)S(1)}, u32[]{:S(2)}) copy-start(f32[192,768]{1,0:T(8,128)S(1)} %bitcast_subtract_fusion) | copy-start | bytes 1769476
Sparse Core Ops, SparseCore 0:
  530.2 47.2 reduce-scatter.1

commit v2 on v1

--- a/solution.py
+++ b/solution.py
@@ -41,12 +41,23 @@
     per = height // depth
     strips = depth // STRIP
     rt = 512 if height % 512 == 0 else 256
+    half = height // 2
+    bits = [1 << n for n in range(chips.bit_length() - 1)]
+    spots = {bit: n for n, bit in enumerate(bits)}
+
+    def onward(x, h):
+        if x == 0:
+            return bits if h == 0 else bits[::-1]
+        return [bit for bit in bits if (bit > x if h == 0 else 2 * bit <= (x & -x))]
+
+    def apart(index):
+        return sum((index // bit + chip // bit) % 2 for bit in bits)
 
     def peer(x):
         return flip(chip, x, chips) * 2 + core
 
     barrier = pltpu.get_barrier_semaphore()
-    for x in range(1, chips):
+    for x in bits:
         pl.semaphore_signal(barrier, inc=1, device_id=(peer(x), row), device_id_type=MESH)
     pl.semaphore_signal(barrier, inc=1, device_id=(mate, row), device_id_type=MESH)
 
@@ -60,11 +71,11 @@
 
     @pl.when((row > 0) & (row < rows - 1))
     def _():
-        pl.semaphore_wait(barrier, chips + 2)
+        pl.semaphore_wait(barrier, len(bits) + 3)
 
     @pl.when((row == 0) | (row == rows - 1))
     def _():
-        pl.semaphore_wait(barrier, chips + 1)
+        pl.semaphore_wait(barrier, len(bits) + 2)
 
     def m_copy(src, j, up):
         return pltpu.make_async_remote_copy(
@@ -73,27 +84,43 @@
             device_id=(sub, row + 1 if up else row - 1), device_id_type=MESH,
         )
 
-    def s_copy(x):
-        return pltpu.make_async_remote_copy(
-            src_ref=s_ref, dst_ref=s_all.at[sub],
-            send_sem=s_send.at[x], recv_sem=s_recv.at[sub],
-            device_id=(peer(x), row), device_id_type=MESH,
-        )
-
-    def s_pass_on(x):
+    def s_half(ref, h):
+        return ref.at[pl.ds(h * half, half)]
+
+    def s_copy(x, bit, h):
         block = peer(x)
         return pltpu.make_async_remote_copy(
-            src_ref=s_ref if x == 0 else s_all.at[block], dst_ref=s_all.at[block],
-            send_sem=s_pass.at[x], recv_sem=s_recv.at[block],
+            src_ref=s_half(s_ref if x == 0 else s_all.at[block], h),
+            dst_ref=s_half(s_all.at[block], h),
+            send_sem=s_send.at[x, spots[bit], h], recv_sem=s_recv.at[block, h],
+            device_id=(peer(bit), row), device_id_type=MESH,
+        )
+
+    def s_pass_on(x, h):
+        block = peer(x)
+        return pltpu.make_async_remote_copy(
+            src_ref=s_half(s_ref if x == 0 else s_all.at[block], h),
+            dst_ref=s_half(s_all.at[block], h),
+            send_sem=s_pass.at[x, h], recv_sem=s_recv.at[block, h],
             device_id=(mate, row), device_id_type=MESH,
         )
 
-    def s_arrived(block):
-        return pltpu.make_async_remote_copy(
-            src_ref=s_all.at[block], dst_ref=s_all.at[block],
-            send_sem=s_send.at[0], recv_sem=s_recv.at[block],
+    def s_arrived(block, h):
+        return pltpu.make_async_remote_copy(
+            src_ref=s_half(s_all.at[block], h), dst_ref=s_half(s_all.at[block], h),
+            send_sem=s_pass.at[0, h], recv_sem=s_recv.at[block, h],
             device_id=(mate, row), device_id_type=MESH,
         )
+
+    def s_receive(x, h):
+        s_arrived(peer(x), h).wait_recv()
+        for bit in onward(x, h):
+            s_copy(x, bit, h).start()
+        s_pass_on(x, h).start()
+
+    def from_mate(x):
+        for h in range(2):
+            s_arrived(flip(chip, x, chips) * 2 + (1 - core), h).wait_recv()
 
     def m_arrived(j):
         return pltpu.make_async_remote_copy(
@@ -110,9 +137,13 @@
         @pl.when(row > 0)
         def _():
             m_copy(m_ref.at[h], row * per + h, False).start()
-    for x in range(1, chips):
-        s_copy(x).start()
-    s_pass_on(0).start()
+
+        if h == 0:
+            for n in range(2):
+                for bit in bits:
+                    s_copy(0, bit, n if bit == bits[0] else 1 - n).start()
+            for n in range(2):
+                s_pass_on(0, n).start()
 
     own_s = pltpu.make_async_copy(s_ref, s_all.at[sub], own_sem.at[0])
     own_m = pltpu.make_async_copy(m_ref, m_all.at[pl.ds(row * per, per)], own_sem.at[1])
@@ -167,34 +198,50 @@
                 + jnp.dot(high, m_high[...], preferred_element_type=jnp.float32)
             )
 
+    def sweep(chosen):
+        @pl.loop(0, subs)
+        def _(j):
+            block = j // per
+            distance = jnp.maximum(block - row, row - block)
+
+            @pl.when(chosen(distance, apart(j // 2)))
+            def _():
+                multiply(j)
+
     near = min(2, rows - 2)
-    for h in range(per):
-        receive(1, h, None)
-    for x in range(1, chips):
-        s_arrived(peer(x)).wait_recv()
-        s_pass_on(x).start()
-    for distance in range(2, near + 1):
-        for h in range(per):
-            receive(distance, h, None)
-    for x in range(chips):
-        s_arrived(flip(chip, x, chips) * 2 + (1 - core)).wait_recv()
-
-    @pl.loop(0, subs)
-    def _(j):
-        block = j // per
-
-        @pl.when((block - row <= near) & (row - block <= near))
-        def _():
-            multiply(j)
+    close = [x for x in range(1, chips) if x in bits]
+    remote = sorted((x for x in range(1, chips) if x not in bits), key=lambda x: x.bit_count())
+    for n in range(2):
+        for x in close:
+            s_receive(x, n if x == bits[0] else 1 - n)
+        for h in range(n, per, 2):
+            receive(1, h, None)
+    from_mate(0)
+    for x in close:
+        from_mate(x)
+    sweep(lambda distance, hops: (distance == 0) & (hops <= 1))
+    for x in remote:
+        for h in range(2):
+            s_receive(x, h)
+    if near > 1:
+        receive(2, 0, None)
+    sweep(lambda distance, hops: (distance == 1) & (hops <= 1))
+    if near > 1:
+        for h in range(1, per):
+            receive(2, h, None)
+    for x in remote:
+        from_mate(x)
+    sweep(lambda distance, hops: (distance <= near) & ((distance > 1) | (hops > 1)))
 
     @pl.loop(0, (rows - 1 - near) * per)
     def _(n):
         receive(near + 1 + n // per, n % per, multiply)
 
-    for x in range(1, chips):
-        s_copy(x).wait_send()
     for x in range(chips):
-        s_pass_on(x).wait_send()
+        for h in range(2):
+            for bit in onward(x, h):
+                s_copy(x, bit, h).wait_send()
+            s_pass_on(x, h).wait_send()
 
     @pl.loop(0, subs)
     def _(j):
@@ -233,9 +280,9 @@
             pltpu.VMEM((depth, width), f32),
             pltpu.VMEM((depth, width), jnp.bfloat16),
             pltpu.VMEM((depth, width), jnp.bfloat16),
-            dma((subs // 2,)),
-            dma((subs // 2,)),
-            dma((subs,)),
+            dma((subs // 2, subs.bit_length(), 2)),
+            dma((subs // 2, 2)),
+            dma((subs, 2)),
             dma((subs,)),
             dma((subs,)),
             dma((subs,)),
@@ -251,6 +298,61 @@
             transcendentals=0,
         ),
     )(strips, sigma_top, coupling.reshape(per, depth, width))[0]
+
+
+def share(subs, rows, own_ref, all_ref, row_send, row_recv, sub_send, sub_recv):
+    sub, row = lax.axis_index("sub"), lax.axis_index("row")
+    barrier = pltpu.get_barrier_semaphore()
+    row_peers = [(sub, (row + d) % rows) for d in range(1, rows)]
+    sub_peers = [((sub + d) % subs, row) for d in range(1, subs)]
+    for peer in row_peers + sub_peers:
+        pl.semaphore_signal(barrier, inc=1, device_id=peer, device_id_type=MESH)
+    pl.semaphore_wait(barrier, rows + subs - 2)
+    all_ref[pl.ds(sub, 1), pl.ds(row, 1)] = own_ref[...][None, None]
+
+    def along_row(d):
+        return pltpu.make_async_remote_copy(
+            src_ref=own_ref, dst_ref=all_ref.at[sub, row],
+            send_sem=row_send.at[d], recv_sem=row_recv.at[d],
+            device_id=row_peers[d], device_id_type=MESH,
+        )
+
+    def along_sub(d):
+        return pltpu.make_async_remote_copy(
+            src_ref=all_ref.at[sub], dst_ref=all_ref.at[sub],
+            send_sem=sub_send.at[d], recv_sem=sub_recv.at[d],
+            device_id=sub_peers[d], device_id_type=MESH,
+        )
+
+    for d in range(rows - 1):
+        along_row(d).start()
+    for d in range(rows - 1):
+        along_row(d).wait()
+    for d in range(subs - 1):
+        along_sub(d).start()
+    for d in range(subs - 1):
+        along_sub(d).wait()
+
+
+def every_variance(subs, rows, own):
+    count = own.shape[0]
+    lanes = -(-count // STRIP) * STRIP
+    padded = jnp.broadcast_to(jnp.pad(own, (0, lanes - count)), (8, lanes))
+    whole = pl.BlockSpec(memory_space=pltpu.VMEM)
+    dma = pltpu.SemaphoreType.DMA
+    shared = pl.pallas_call(
+        functools.partial(share, subs, rows),
+        out_shape=jax.ShapeDtypeStruct((subs, rows, 8, lanes), jnp.float32),
+        in_specs=[whole],
+        out_specs=whole,
+        scratch_shapes=[
+            dma((rows - 1,)), dma((rows - 1,)), dma((subs - 1,)), dma((subs - 1,)),
+        ],
+        compiler_params=pltpu.CompilerParams(
+            collective_id=1, has_side_effects=True, vmem_limit_bytes=16 * 2**20
+        ),
+    )(padded)
+    return shared[:, :, 0, :count].reshape(-1)
 
 
 def local(subs, rows, sigma_top, coupling, child_inverse, tile_mask, obs_node, obs_noise):
@@ -277,7 +379,7 @@
     block_here = child_inverse[0] - update
     own_cols = lax.dynamic_slice_in_dim(block_here, row_index * width_here, width_here, 1)
     own_diag = jnp.diagonal(own_cols)
-    every_var = lax.all_gather(own_diag, ("sub", "row"), axis=0, tiled=True)
+    every_var = every_variance(subs, rows, own_diag)
     loo_var = every_var[obs_node] + obs_noise
     return (sep_part[None], block_here[None], loo_var)
 

time: 630 us -> 601 us (0.954)
  blocking collectives: 39.9 us -> 0 us
  Pallas kernels: 509 us -> 519 us
    unnamed x1 -> x0, blocking collectives: 39.9 us -> none
    pallas_call x0 -> x1, Pallas kernels: none -> 9.97 us  [every_variance(): pl.pallas_call(functools.partial(share, subs, rows), out_shape=jax.ShapeD...]
where the time goes in v2:
time: 601 us; the launch traced here: 600 us
  Pallas kernels  519 us (86%)
  waiting for transfers between devices  43.4 us (7%)
  between operations  14.2 us (2%)
  matrix products  10.8 us (2%)
  other arithmetic  8.01 us (1%)
    pallas_call x1, Pallas kernels, product_here(): pl.pallas_call(functools.partial(gather_multiply, subs, rows), out_shape=...  509 us
    reduce_scatter x1, waiting for transfers between devices, local(): lax.psum_scatter(lax.dot_general(masked, sep_part, (((0,), (0,)), ((), ()...  43.4 us
  transfers between devices with their start and end apart: 1, of which 1 were waited for; matrix products, arithmetic and copies ran while one was open for 1% of the time, Pallas kernels for 0%

profile of v2, /device:TPU:0, one launch (start us, length us, event | category | flops | bytes accessed | tf_op | source)
XLA Modules:
  0.0 600.5 jit_solution(1775851914113465679)
XLA Ops:
  7.2 0.0 reduce-scatter.2.cloned.1.call-start
  7.2 0.7 convert_bitcast_fusion.1
  7.9 0.1 broadcast_in_dim.29
  7.9 0.1 convert_element_type.32
  8.0 0.7 convert_bitcast_fusion
  8.8 0.1 broadcast_in_dim.32
  8.9 1.2 broadcast_in_dim.30.mask_ref
  10.0 0.0 copy-start.4
  10.0 508.8 %shard_map.85 = (f32[1536,768]{1,0:T(8,128)}, f32[8,1536,768]{2,1,0:T(8,128)}, f32[8,768,768]{2,1,0:T(8,128)}) custom-call(f32[48,8,768]{2,1,0:T(8,128)} %broadcast_in_dim.30.mask_ref, f32[1536,768]{1,0:T(8,128)} %s_ref.1, f32[2,768,768]{2,1,0:T(8,128)} %bitcast.16), custom_call_target="tpu_custom_call" | custom-call | flops 43486543872 | bytes 113246208 | tf_op jit(solution)/shard_map/pallas_call | solution.py:269
  518.8 0.0 copy-done.4
  518.8 0.0 copy-start.3
  518.8 10.8 %fusion = f32[768,768]{1,0:T(8,128)} fusion(f32[1,1536,768]{2,1,0:T(8,128)S(1)} %copy-done.4, f32[1536,768]{1,0:T(8,128)} %get-tuple-element.4, f32[1536]{0:T(1024)S(1)} %convert_element_type.35), kind=kOutput, calls=%fused_computation.3 | convolution fusion | flops 5438177280 | bytes 11802624 | tf_op jit(solution)/shard_map/dot_general | solution.py:368
  529.6 0.0 reduce-scatter.2.cloned.1.call-update
  529.6 0.0 copy-done.3
  529.6 0.0 copy-start.1
  529.7 4.9 negate_bitcast_fusion
  534.5 0.0 copy-start.2
  534.5 43.4 %reduce-scatter.2.cloned.1.call-done = f32[192,768]{1,0:T(8,128)} async-done(((f32[768,768]{1,0:T(8,128)}), f32[192,768]{1,0:T(8,128)}) %reduce-scatter.2.cloned.1.call-update) | async-done | bytes 589840 | tf_op jit(solution)/shard_map/reduce_scatter | solution.py:367
  577.9 0.0 copy-done.1
  577.9 1.1 bitcast_subtract_fusion
  579.1 0.0 copy-start
  579.1 0.1 constant_dynamic-slice_fusion
  579.2 1.9 gather_fusion
  581.1 10.0 %shard_map.86 = f32[8,4,8,256]{3,2,1,0:T(8,128)S(1)} custom-call(f32[8,256]{1,0:T(8,128)S(1)} %broadcast_in_dim.34.own_ref), custom_call_target="tpu_custom_call" | custom-call | tf_op jit(solution)/shard_map/pallas_call | solution.py:343
  591.1 0.1 slice_reduce_fusion
  591.2 0.1 reshape_squeeze.7
  591.3 1.7 gather_fusion.1
  593.0 0.0 copy-done.2
  593.1 0.6 add.27
  593.6 0.0 copy-done
  (6 shorter events, 0.0 us)
Async XLA Ops:
  7.2 570.8 %reduce-scatter.2.cloned.1.call-start = ((), (), s32[]{:S(2)}) async-start(), calls=%async_computation.1 | async-start | bytes 2949120 | tf_op jit(solution)/shard_map/reduce_scatter | solution.py:367
  10.0 508.8 %copy-start.4 = (f32[1,1536,768]{2,1,0:T(8,128)S(1)}, f32[1,1536,768]{2,1,0:T(8,128)}, u32[]{:S(2)}) copy-start(f32[1,1536,768]{2,1,0:T(8,128)} %param.7) | copy-start | bytes 14155780
  518.8 10.8 %copy-start.3 = (s32[256]{0:T(256)S(1)}, s32[256]{0:T(256)}, u32[]{:S(2)}) copy-start(s32[256]{0:T(256)} %param.10) | copy-start | bytes 3076
  529.6 48.3 %copy-start.1 = (f32[1,192,768]{2,1,0:T(8,128)S(1)}, f32[1,192,768]{2,1,0:T(8,128)}, u32[]{:S(2)}) copy-start(f32[1,192,768]{2,1,0:T(8,128)} %param.8) | copy-start | bytes 1769476
  534.5 58.5 %copy-start.2 = (f32[256]{0:T(256)S(1)}, f32[256]{0:T(256)}, u32[]{:S(2)}) copy-start(f32[256]{0:T(256)} %param.11) | copy-start | bytes 3076
  579.1 14.6 %copy-start = (f32[192,768]{1,0:T(8,128)}, f32[192,768]{1,0:T(8,128)S(1)}, u32[]{:S(2)}) copy-start(f32[192,768]{1,0:T(8,128)S(1)} %bitcast_subtract_fusion) | copy-start | bytes 1769476
Sparse Core Ops, SparseCore 0:
  529.7 48.1 reduce-scatter.1
